TPU v7x, 256 devices: a whole 4x4x8 slice. The times are simulated.
256 devices in a mesh: dp: 8 (over z_lo, y), expert: 32 (over z_hi, x, core).
Axes of the slice: x: 4, y: 4, z: 8 (z_hi: 4, z_lo: 2; z = z_hi * 2 + z_lo), core: 2. Of those that a mesh axis runs over, the one named last changes fastest.
Arguments:
- tokens: bfloat16 [32768, 2048], P(('dp', 'expert')), may hold values from -6 to 6
- grad_out: bfloat16 [32768, 2048], P(('dp', 'expert')), may hold values from -1.5 to 1.5
- routes: int32 [32768, 2], P(('dp', 'expert')), may hold values from 0 to 31, all different within a row; in each aligned block of 128 rows (0 to 127, 128 to 255, ...) at most 16 rows name the same one
- gate_fixed: int32 [32768, 2], P(('dp', 'expert')), may hold values from 26 to 256
- live_count: int32 [256], P(('dp', 'expert')), may hold values from 1 to 128, 28672 in all
- w_gate: bfloat16 [32, 2048, 768], P('expert', 'dp'), may hold values from -0.125 to 0.125
- w_up: bfloat16 [32, 2048, 768], P('expert', 'dp'), may hold values from -0.125 to 0.125
- w_down: bfloat16 [32, 768, 2048], P('expert', None, 'dp'), may hold values from -0.21875 to 0.21875
Outputs:
- d_tokens: bfloat16 [32768, 2048], P(('dp', 'expert'))
- d_gates: bfloat16 [32768, 2], P(('dp', 'expert'))
- grad_gate: bfloat16 [32, 2048, 768], P('expert', 'dp')
- grad_up: bfloat16 [32, 2048, 768], P('expert', 'dp')
- grad_down: bfloat16 [32, 768, 2048], P('expert', None, 'dp')
Inputs may be any that keep to these rules, and one draw needn't show every extreme that they name: `routes`: each row names 2 different experts; among the rows of one device no expert is named more than 16 times. `live_count`: a device's live tokens are its first rows; the largest count equals 128.
All inputs are finite; a program needn't handle non-finite values.
Results may differ from a plain program's by a relative error of at most 0.017.
Values may be sent and summed in bfloat16 or wider, within the bound.
No kernel may reach another device: no remote copies, remote signals or barrier semaphores. Data moves between devices by JAX's collectives and lax.ppermute only.
A program may use at most 128 MiB of HBM per device.

v0:
```python
import jax
import jax.numpy as jnp
from jax import lax
from jax.sharding import PartitionSpec as P


def contract_last(left, right):
    return lax.dot_general(
        left, right, (((1,), (1,)), ((), ())), preferred_element_type=jnp.float32
    )


def contract_first(left, right):
    return lax.dot_general(
        left, right, (((0,), (0,)), ((), ())), preferred_element_type=jnp.float32
    )


def local(tokens, grad_out, routes, gate_fixed, live_count, w_gate, w_up, w_down):
    tok_rows, top_routes = routes.shape
    feature_width = tokens.shape[1]
    hidden_units = w_gate.shape[2]
    experts = w_gate.shape[0] * lax.axis_size("expert")
    capacity = 2 * tok_rows * top_routes // experts
    slot_total = experts * capacity
    flat_routes = routes.reshape(-1)
    live_routes = jnp.repeat(jnp.arange(tok_rows, dtype=jnp.int32) < live_count[0], top_routes)
    matches = (
        (flat_routes[:, None] == jnp.arange(experts, dtype=jnp.int32)[None, :])
        & live_routes[:, None]
    ).astype(jnp.int32)
    slot_rank = jnp.sum((jnp.cumsum(matches, axis=0) - matches) * matches, axis=1)
    slot_index = jnp.where(live_routes, flat_routes * capacity + slot_rank, slot_total)
    token_of = jnp.arange(tok_rows * top_routes, dtype=jnp.int32) // top_routes
    gate_values = (gate_fixed.reshape(-1).astype(jnp.float32) / 256.0).astype(jnp.bfloat16)
    inputs_send = (
        jnp.zeros((slot_total, feature_width), jnp.bfloat16)
        .at[slot_index]
        .set(tokens[token_of], mode="drop")
    )
    inputs_send = inputs_send.reshape(experts, capacity, feature_width)
    grads_send = (
        jnp.zeros((slot_total, feature_width), jnp.bfloat16)
        .at[slot_index]
        .set(grad_out[token_of], mode="drop")
    )
    grads_send = grads_send.reshape(experts, capacity, feature_width)
    gates_send = (
        jnp.zeros((slot_total,), jnp.bfloat16)
        .at[slot_index]
        .set(gate_values, mode="drop")
        .reshape(experts, capacity)
    )
    inputs_recv, grads_recv, gates_recv = (
        lax.all_to_all(inputs_send, "expert", split_axis=0, concat_axis=0, tiled=True),
        lax.all_to_all(grads_send, "expert", split_axis=0, concat_axis=0, tiled=True),
        lax.all_to_all(gates_send, "expert", split_axis=0, concat_axis=0, tiled=True),
    )
    inputs_rows = inputs_recv.reshape(slot_total, feature_width)
    local_gate = w_gate[0]
    local_up = w_up[0]
    local_down = w_down[0]
    columns = inputs_rows
    gate_pre = jnp.dot(
        columns,
        lax.all_gather(local_gate, "dp", axis=0, tiled=True),
        preferred_element_type=jnp.float32,
    )
    up_pre = jnp.dot(
        columns,
        lax.all_gather(local_up, "dp", axis=0, tiled=True),
        preferred_element_type=jnp.float32,
    )
    grads_rows = grads_recv.reshape(slot_total, feature_width)
    gate_scale = gates_recv.reshape(slot_total, 1).astype(jnp.float32)
    sigmoid_val = jax.nn.sigmoid(gate_pre)
    activated = gate_pre * sigmoid_val
    hidden = activated * up_pre
    columns = grads_rows
    back_hidden = contract_last(columns, lax.all_gather(local_down, "dp", axis=1, tiled=True))
    route_grad = jnp.sum(back_hidden * hidden, axis=1).astype(jnp.bfloat16)
    scaled = gate_scale * back_hidden
    up_delta = (scaled * activated).astype(jnp.bfloat16)
    gate_delta = (scaled * up_pre * sigmoid_val * (1.0 + gate_pre * (1.0 - sigmoid_val))).astype(
        jnp.bfloat16
    )
    weighted = (gate_scale * hidden).astype(jnp.bfloat16)
    stacked = jnp.stack([local_gate, local_up])
    piece = lax.all_gather(stacked, "dp", axis=1, tiled=True)
    slot_dx = (contract_last(gate_delta, piece[0]) + contract_last(up_delta, piece[1])).astype(
        jnp.bfloat16
    )
    summed = lax.psum_scatter(
        jnp.concatenate(
            [
                contract_first(inputs_rows, gate_delta),
                contract_first(inputs_rows, up_delta),
                contract_first(grads_rows, weighted),
            ],
            axis=1,
        ).astype(jnp.bfloat16),
        "dp",
        scatter_dimension=0,
        tiled=True,
    ).astype(jnp.float32)
    grad_gate = summed[:, :hidden_units].astype(jnp.bfloat16)[None]
    grad_up = summed[:, hidden_units : 2 * hidden_units].astype(jnp.bfloat16)[None]
    grad_down = summed[:, 2 * hidden_units :].T.astype(jnp.bfloat16)[None]
    returned_dx, returned_gate = (
        lax.all_to_all(
            slot_dx.reshape(experts, capacity, feature_width),
            "expert",
            split_axis=0,
            concat_axis=0,
            tiled=True,
        ),
        lax.all_to_all(
            route_grad.reshape(experts, capacity), "expert", split_axis=0, concat_axis=0, tiled=True
        ),
    )
    back_rows = jnp.take(
        returned_dx.reshape(slot_total, feature_width),
        slot_index,
        axis=0,
        mode="fill",
        fill_value=0,
    )
    token_grads = jnp.sum(
        back_rows.astype(jnp.float32).reshape(tok_rows, top_routes, feature_width), axis=1
    ).astype(jnp.bfloat16)
    gate_grads = jnp.take(
        returned_gate.reshape(-1), slot_index, axis=0, mode="fill", fill_value=0
    ).reshape(tok_rows, top_routes)
    return (token_grads, gate_grads, grad_gate, grad_up, grad_down)


def solution(mesh):
    return jax.shard_map(
        local,
        mesh=mesh,
        in_specs=(
            P(("dp", "expert"), None),
            P(("dp", "expert"), None),
            P(("dp", "expert"), None),
            P(("dp", "expert"), None),
            P(("dp", "expert")),
            P("expert", "dp", None),
            P("expert", "dp", None),
            P("expert", None, "dp"),
        ),
        out_specs=(
            P(("dp", "expert"), None),
            P(("dp", "expert"), None),
            P("expert", "dp", None),
            P("expert", "dp", None),
            P("expert", None, "dp"),
        ),
        check_vma=False,
    )
```

profile of v0, /device:TPU:1, one launch (start us, length us, event | category | flops | bytes accessed | tf_op | source)
XLA Modules:
  0.0 470.2 jit_solution(688029951581968453)
XLA Ops:
  13.9 2.2 scatter_custom_fusion
  16.7 12.6 %all-to-all-start = ((bf16[32,1,16]{2,1,0:T(2,128)(2,1)}), bf16[32,1,16]{2,1,0:T(2,128)(2,1)S(1)}, u32[]{:S(2)}, u32[]{:S(2)}) async-start(bf16[32,1,16]{2,1,0:T(2,128)(2,1)} %all_to_all.25), calls=%async_computation | async-start | bytes 32768 | tf_op jit(solution)/shard_map/all_to_all | solution.py:57
  29.4 7.0 %scatter_custom_fusion.2 = bf16[512,2048]{1,0:T(8,128)(2,1)} fusion(s32[256]{0:T(256)S(1)} %bitcast.76, bf16[128,2048]{1,0:T(8,128)(2,1)S(1)} %copy-done, s32[1024]{0:T(1024)S(1)} %pad_clamp_fusion.1, bf16[]{:T(256)} %constant.60.clone.1), kind=kCustom, calls=%fused_computation.30 | custom fusion | bytes 2097154 | tf_op jit(solution)/shard_map/scatter | solution.py:39
  36.4 2.3 all-to-all-done
  38.6 7.6 %all-to-all-start.2 = ((bf16[32,16,2048]{2,1,0:T(8,128)(2,1)}), bf16[32,16,2048]{2,1,0:T(8,128)(2,1)S(1)}, u32[]{:S(2)}, u32[]{:S(2)}) async-start(bf16[32,16,2048]{2,1,0:T(8,128)(2,1)} %bitcast.8), calls=%async_computation.2 | async-start | bytes 4194304 | tf_op jit(solution)/shard_map/all_to_all | solution.py:55
  46.5 1.0 pad_maximum_fusion.1
  47.5 7.2 %scatter_custom_fusion.1 = bf16[512,2048]{1,0:T(8,128)(2,1)} fusion(s32[256]{0:T(256)S(1)} %bitcast.77, bf16[128,2048]{1,0:T(8,128)(2,1)} %param.9, s32[1024]{0:T(1024)S(1)} %pad_clamp_fusion.1, bf16[]{:T(256)} %constant.60.clone.1), kind=kCustom, calls=%fused_computation.32 | custom fusion | bytes 2097664 | tf_op jit(solution)/shard_map/scatter | solution.py:45
  54.7 50.4 %all-to-all-done.2 = bf16[32,16,2048]{2,1,0:T(8,128)(2,1)S(1)} async-done(((bf16[32,16,2048]{2,1,0:T(8,128)(2,1)}), bf16[32,16,2048]{2,1,0:T(8,128)(2,1)S(1)}, u32[]{:S(2)}, u32[]{:S(2)}) %all-to-all-start.2) | async-done | bytes 2097184 | tf_op jit(solution)/shard_map/all_to_all | solution.py:55
  105.1 8.8 %all-to-all-start.1 = ((bf16[32,16,2048]{2,1,0:T(8,128)(2,1)}), bf16[32,16,2048]{2,1,0:T(8,128)(2,1)}, u32[]{:S(2)}, u32[]{:S(2)}) async-start(bf16[32,16,2048]{2,1,0:T(8,128)(2,1)} %bitcast.5), calls=%async_computation.1 | async-start | bytes 4194304 | tf_op jit(solution)/shard_map/all_to_all | solution.py:56
  114.1 4.9 %fusion.2 = f32[512,768]{1,0:T(8,128)} fusion(bf16[512,2048]{1,0:T(8,128)(2,1)S(1)} %bitcast.69, bf16[1,2048,768]{2,1,0:T(8,128)(2,1)} %all-gather.14.cloned.1.call-done), kind=kOutput, calls=%fused_computation.16 | convolution fusion | flops 1610612736 | bytes 6815744 | tf_op jit(solution)/shard_map/dot_general | solution.py:64
  119.0 54.5 %all-gather.12.cloned.1.call-done = bf16[1,2048,768]{2,1,0:T(8,128)(2,1)} async-done(((bf16[1,256,768]{2,1,0:T(8,128)(2,1)}), bf16[1,2048,768]{2,1,0:T(8,128)(2,1)}) %all-gather.12.cloned.1.call-update) | async-done | bytes 3145744 | tf_op jit(solution)/shard_map/all_gather | solution.py:71
  173.4 4.8 %fusion.4 = f32[512,768]{1,0:T(8,128)} fusion(bf16[512,2048]{1,0:T(8,128)(2,1)S(1)} %bitcast.70, bf16[1,2048,768]{2,1,0:T(8,128)(2,1)} %all-gather.12.cloned.1.call-done), kind=kOutput, calls=%fused_computation.18 | convolution fusion | flops 1610612736 | bytes 6815744 | tf_op jit(solution)/shard_map/dot_general | solution.py:69
  178.3 2.3 all-to-all-done.1
  180.6 47.7 %all-gather.10.cloned.1.call-done = bf16[1,768,2048]{2,1,0:T(8,128)(2,1)} async-done(((bf16[1,768,256]{2,1,0:T(8,128)(2,1)}), bf16[1,768,2048]{2,1,0:T(8,128)(2,1)}) %all-gather.10.cloned.1.call-update) | async-done | bytes 3145744 | tf_op jit(solution)/shard_map/all_gather | solution.py:80
  228.2 5.9 %multiply_reduce_fusion = (bf16[512]{0:T(512)(128)(2,1)S(1)}, bf16[512,768]{1,0:T(8,128)(2,1)S(1)}, bf16[512,768]{1,0:T(8,128)(2,1)S(1)}) fusion(f32[512,768]{1,0:T(8,128)} %fusion.4, f32[512,768]{1,0:T(8,128)} %fusion.2, f32[512]{0:T(512)S(1)} %reshape.212, bf16[512,2048]{1,0:T(8,128)(2,1)} %bitcast.6, bf16[1,768,2048]{2,1,0:T(8,128)(2,1)} %all-gather.10.cloned.1.call-done), kind=kOutput, calls=%fused_computation.24 | convolution fusion | flops 1617296896 | bytes 9964544 | tf_op jit(solution)/shard_map/dot_general | solution.py:8
  234.2 1.9 convolution_convert_fusion.1
  236.1 1.9 convolution_convert_fusion.2
  238.0 3.6 convolution_convert_fusion
  241.6 4.5 pad_maximum_fusion
  246.8 12.7 %all-to-all-start.4 = ((bf16[32,1,16]{2,1,0:T(2,128)(2,1)}), bf16[32,1,16]{2,1,0:T(2,128)(2,1)S(1)}, u32[]{:S(2)}, u32[]{:S(2)}) async-start(bf16[32,1,16]{2,1,0:T(2,128)(2,1)} %convert_element_type.80), calls=%async_computation.4 | async-start | bytes 32768 | tf_op jit(solution)/shard_map/all_to_all | solution.py:117
  259.6 49.1 %all-gather.8.cloned.1.call-done = bf16[2,2048,768]{2,1,0:T(8,128)(2,1)} async-done(((bf16[2,256,768]{2,1,0:T(8,128)(2,1)}), bf16[2,2048,768]{2,1,0:T(8,128)(2,1)}) %all-gather.8.cloned.1.call-update) | async-done | bytes 6291472 | tf_op jit(solution)/shard_map/all_gather | solution.py:89
  308.7 3.9 fusion
  312.6 3.2 add_convert_fusion
  315.8 9.4 %all-to-all-start.3 = ((bf16[32,16,2048]{2,1,0:T(8,128)(2,1)}), bf16[32,16,2048]{2,1,0:T(8,128)(2,1)S(1)}, u32[]{:S(2)}, u32[]{:S(2)}) async-start(bf16[32,16,2048]{2,1,0:T(8,128)(2,1)} %bitcast.73), calls=%async_computation.3 | async-start | bytes 4194304 | tf_op jit(solution)/shard_map/all_to_all | solution.py:110
  325.4 1.9 gather_fusion.1
  328.3 70.9 %all-to-all-done.3 = bf16[32,16,2048]{2,1,0:T(8,128)(2,1)S(1)} async-done(((bf16[32,16,2048]{2,1,0:T(8,128)(2,1)}), bf16[32,16,2048]{2,1,0:T(8,128)(2,1)S(1)}, u32[]{:S(2)}, u32[]{:S(2)}) %all-to-all-start.3) | async-done | bytes 2097184 | tf_op jit(solution)/shard_map/all_to_all | solution.py:110
  399.1 2.3 gather_fusion
  401.4 1.7 gather.21
  403.2 3.1 fusion.9
  406.2 53.5 %reduce-scatter.2.cloned.1.call-done = bf16[256,2304]{0,1:T(8,128)(2,1)} async-done(((bf16[2048,2304]{0,1:T(8,128)(2,1)}), bf16[256,2304]{0,1:T(8,128)(2,1)}) %reduce-scatter.2.cloned.1.call-update) | async-done | bytes 1179664 | tf_op jit(solution)/shard_map/reduce_scatter | solution.py:93
  459.8 2.1 slice_bitcast_fusion.6
  461.8 0.9 copy.32
  (64 shorter events, 9.8 us)
Async XLA Ops:
  7.2 22.2 %copy-start = (bf16[128,2048]{1,0:T(8,128)(2,1)S(1)}, bf16[128,2048]{1,0:T(8,128)(2,1)}, u32[]{:S(2)}) copy-start(bf16[128,2048]{1,0:T(8,128)(2,1)} %param.8) | copy-start | bytes 1572868
  7.2 106.9 %all-gather.14.cloned.1.call-start = ((), (), s32[]{:S(2)}) async-start(), calls=%async_computation.10 | async-start | bytes 3538944 | tf_op jit(solution)/shard_map/all_gather | solution.py:66
  7.9 165.5 %all-gather.12.cloned.1.call-start = ((), (), s32[]{:S(2)}) async-start(), calls=%async_computation.9 | async-start | bytes 3538944 | tf_op jit(solution)/shard_map/all_gather | solution.py:71
  8.7 219.6 %all-gather.10.cloned.1.call-start = ((), (), s32[]{:S(2)}) async-start(), calls=%async_computation.8 | async-start | bytes 3538944 | tf_op jit(solution)/shard_map/all_gather | solution.py:80
  16.7 21.9 %all-to-all-start = ((bf16[32,1,16]{2,1,0:T(2,128)(2,1)}), bf16[32,1,16]{2,1,0:T(2,128)(2,1)S(1)}, u32[]{:S(2)}, u32[]{:S(2)}) async-start(bf16[32,1,16]{2,1,0:T(2,128)(2,1)} %all_to_all.25), calls=%async_computation | async-start | bytes 32768 | tf_op jit(solution)/shard_map/all_to_all | solution.py:57
  38.6 7.9 %copy-start.1 = (bf16[1,256,768]{2,1,0:T(8,128)(2,1)S(1)}, bf16[1,256,768]{2,1,0:T(8,128)(2,1)}, u32[]{:S(2)}) copy-start(bf16[1,256,768]{2,1,0:T(8,128)(2,1)} %param.13) | copy-start | bytes 1179652
  38.6 7.9 %copy-start.2 = (bf16[1,256,768]{2,1,0:T(8,128)(2,1)S(1)}, bf16[1,256,768]{2,1,0:T(8,128)(2,1)}, u32[]{:S(2)}) copy-start(bf16[1,256,768]{2,1,0:T(8,128)(2,1)} %param.14) | copy-start | bytes 1179652
  38.6 66.5 %all-to-all-start.2 = ((bf16[32,16,2048]{2,1,0:T(8,128)(2,1)}), bf16[32,16,2048]{2,1,0:T(8,128)(2,1)S(1)}, u32[]{:S(2)}, u32[]{:S(2)}) async-start(bf16[32,16,2048]{2,1,0:T(8,128)(2,1)} %bitcast.8), calls=%async_computation.2 | async-start | bytes 4194304 | tf_op jit(solution)/shard_map/all_to_all | solution.py:55
  46.3 262.4 %all-gather.8.cloned.1.call-start = ((), (), s32[]{:S(2)}) async-start(), calls=%async_computation.6 | async-start | bytes 7077888 | tf_op jit(solution)/shard_map/all_gather | solution.py:89
  105.1 75.5 %all-to-all-start.1 = ((bf16[32,16,2048]{2,1,0:T(8,128)(2,1)}), bf16[32,16,2048]{2,1,0:T(8,128)(2,1)}, u32[]{:S(2)}, u32[]{:S(2)}) async-start(bf16[32,16,2048]{2,1,0:T(8,128)(2,1)} %bitcast.5), calls=%async_computation.1 | async-start | bytes 4194304 | tf_op jit(solution)/shard_map/all_to_all | solution.py:56
  113.9 345.9 %reduce-scatter.2.cloned.1.call-start = ((), (), s32[]{:S(2)}) async-start(), calls=%async_computation.7 | async-start | bytes 10616832 | tf_op jit(solution)/shard_map/reduce_scatter | solution.py:93
  234.2 1.9 copy-start.4
  236.1 1.9 copy-start.6
  236.1 1.9 copy-start.7
  246.1 62.6 %copy-start.5 = (bf16[512,768]{1,0:T(8,128)(2,1)S(1)}, bf16[512,768]{1,0:T(8,128)(2,1)}, u32[]{:S(2)}) copy-start(bf16[512,768]{1,0:T(8,128)(2,1)} %copy-done.4) | copy-start | bytes 2359300
  246.8 68.9 %all-to-all-start.4 = ((bf16[32,1,16]{2,1,0:T(2,128)(2,1)}), bf16[32,1,16]{2,1,0:T(2,128)(2,1)S(1)}, u32[]{:S(2)}, u32[]{:S(2)}) async-start(bf16[32,1,16]{2,1,0:T(2,128)(2,1)} %convert_element_type.80), calls=%async_computation.4 | async-start | bytes 32768 | tf_op jit(solution)/shard_map/all_to_all | solution.py:117
  308.7 3.9 copy-start.3
  315.8 83.3 %all-to-all-start.3 = ((bf16[32,16,2048]{2,1,0:T(8,128)(2,1)}), bf16[32,16,2048]{2,1,0:T(8,128)(2,1)S(1)}, u32[]{:S(2)}, u32[]{:S(2)}) async-start(bf16[32,16,2048]{2,1,0:T(8,128)(2,1)} %bitcast.73), calls=%async_computation.3 | async-start | bytes 4194304 | tf_op jit(solution)/shard_map/all_to_all | solution.py:110
Sparse Core Ops, SparseCore 0:
  9.8 70.1 all-gather.13
  81.8 91.5 all-gather.11
  175.2 53.0 all-gather.9
  229.9 78.7 all-gather.7
  311.1 148.6 reduce-scatter.1
where the time goes:
time: 471 us; the launch traced here: 470 us
  waiting for transfers between devices  333 us (71%)
  starting transfers between devices  51.5 us (11%)
  local copies, waits for them, and re-layouts  31 us (7%)
  matrix products  30.1 us (6%)
  between operations  14.7 us (3%)
  other arithmetic  10.2 us (2%)
    all_to_all x1, waiting for transfers between devices, local(): lax.all_to_all(slot_dx.reshape(experts, capacity, feature_width), 'expert...  70.9 us
    all_gather x1, waiting for transfers between devices, local(): lax.all_gather(local_up, 'dp', axis=0, tiled=True)  54.5 us
    reduce_scatter x1, waiting for transfers between devices, local(): lax.psum_scatter(jnp.concatenate([contract_first(inputs_rows, gate_delta)...  53.5 us
    all_to_all x1, waiting for transfers between devices, local(): lax.all_to_all(inputs_send, 'expert', split_axis=0, concat_axis=0, tiled=...  50.4 us
    all_gather x1, waiting for transfers between devices, local(): piece = lax.all_gather(stacked, 'dp', axis=1, tiled=True)  49.1 us
    all_gather x1, waiting for transfers between devices, local(): lax.all_gather(local_down, 'dp', axis=1, tiled=True)  47.7 us
    dot_general x3, matrix products, contract_last(): lax.dot_general(left, right, (((1,), (1,)), ((), ())), preferred_element_...  13 us
    all_to_all x1, starting transfers between devices, local(): lax.all_to_all(route_grad.reshape(experts, capacity), 'expert', split_axi...  12.7 us
  transfers between devices with their start and end apart: 10, of which 8 were waited for; matrix products, arithmetic and copies ran while one was open for 14% of the time, Pallas kernels for 0%

commit v1 on v0

v1 whole, which is shorter than its diff:
```python
import jax
import jax.numpy as jnp
from jax import lax
from jax.sharding import PartitionSpec as P

NZ, NY, NX = 8, 4, 4
ALL = ("dp", "expert")
CAP = 16
GROUP = 2 * NX


def place(index):
    dp, expert = divmod(index, (NZ // 2) * GROUP)
    z_lo, y = divmod(dp, NY)
    z_hi, rest = divmod(expert, GROUP)
    x, core = divmod(rest, 2)
    return 2 * z_hi + z_lo, y, x, core


def index_of(z, y, x, core):
    z, y, x = z % NZ, y % NY, x % NX
    return ((z % 2) * NY + y) * (NZ // 2) * GROUP + (z // 2) * GROUP + x * 2 + core


def move(array, to):
    pairs = [(i, index_of(*to(*place(i)))) for i in range(NZ * NY * GROUP)]
    return lax.ppermute(array, ALL, pairs)


def across(z, y, x, core):
    return (z + 1 if z % 2 else z - 1), y, x, core


def onward(z, y, x, core):
    return (z - 2 if z % 2 else z + 2), y, x, core


def backward(z, y, x, core):
    return (z + 2 if z % 2 else z - 2), y, x, core


def twin(z, y, x, core):
    return z ^ 1, y, x, core


def y_by(step):
    return lambda z, y, x, core: (z, y + step, x, core)


def x_by(step, flip):
    return lambda z, y, x, core: (z, y, x + step, core ^ flip)


def dot(left, right, dims):
    return lax.dot_general(left, right, (dims, ((), ())), preferred_element_type=jnp.float32)


def bf16(array):
    return array.astype(jnp.bfloat16)


def f32(array):
    return array.astype(jnp.float32)


def hold(array, *after):
    return lax.optimization_barrier((array,) + after)[0]


def local(tokens, grad_out, routes, gate_fixed, live_count, w_gate, w_up, w_down):
    rows, width = tokens.shape
    hidden_units = w_gate.shape[2]
    shard = w_gate.shape[1]
    half = shard // 2
    dp = lax.axis_index("dp")
    expert = lax.axis_index("expert")
    z_lo, y = dp // NY, dp % NY
    z_hi, x, core = expert // GROUP, (expert % GROUP) // 2, expert % 2

    live = jnp.arange(rows, dtype=jnp.int32)[None, :] < live_count[0]
    meta = jnp.concatenate([jnp.where(live, routes.T, -1), gate_fixed.T], axis=0)
    meta_near = jnp.stack([meta, move(meta, across)])
    meta_all = jnp.concatenate([meta_near, move(meta_near, onward)])

    tok_near = move(tokens, across)
    tok_far = move(tokens, onward)
    tok_last = move(tok_near, onward)
    grad_first = hold(grad_out, tok_near)
    grad_near = move(grad_first, across)
    grad_far = move(grad_first, onward)
    grad_last = move(grad_near, onward)

    own = jnp.stack([w_gate[0], w_up[0], w_down[0].T])
    other = move(own, twin)
    gathered = []
    for block in (own, other):
        from_left = move(block, y_by(1))
        from_right = move(block, y_by(-1))
        far_top = move(from_left[:, :half], y_by(1))
        far_low = move(from_right[:, half:], y_by(-1))
        gathered.append((block, from_right, (far_top, far_low), from_left))
    full = []
    for at in range(3):
        whole = jnp.zeros((2 * NY * shard, hidden_units), jnp.bfloat16)
        for far_z in range(2):
            for dy in range(NY):
                start = (((z_lo + far_z) % 2) * NY + (y + dy) % NY) * shard
                block = gathered[far_z][dy]
                if dy == 2:
                    whole = lax.dynamic_update_slice(whole, block[0][at], (start, 0))
                    whole = lax.dynamic_update_slice(whole, block[1][at], (start + half, 0))
                else:
                    whole = lax.dynamic_update_slice(whole, block[at], (start, 0))
        full.append(whole)
    full_gate, full_up, full_down = full

    destinations = [(dx, flip) for dx in range(NX) for flip in range(2)]
    wanted = jnp.stack([z_hi * GROUP + ((x + dx) % NX) * 2 + (core ^ flip) for dx, flip in destinations])
    route_a, route_b = meta_all[:, 0], meta_all[:, 1]
    hit_a = route_a[None] == wanted[:, None, None]
    hit_b = route_b[None] == wanted[:, None, None]
    hit = (hit_a | hit_b).astype(jnp.bfloat16)
    before = (jnp.arange(rows)[:, None] < jnp.arange(rows)[None, :]).astype(jnp.bfloat16)
    rank = dot(hit, before, ((2,), (0,)))
    ranks = jnp.arange(CAP, dtype=jnp.float32)[None, None, :, None]
    chosen = (rank[:, :, None, :] == ranks) & (hit[:, :, None, :] > 0)
    sources = meta_all.shape[0]
    same = jnp.eye(sources, dtype=jnp.bool_)[None, :, None, :, None]

    def spread(mask, values):
        wide = jnp.where(mask[:, :, :, None, :] & same, values, 0)
        return bf16(wide).reshape(len(destinations) * sources * CAP, sources * rows)

    gates = f32(meta_all[:, 2:]) / 256.0
    gate_of = jnp.where(hit_a, gates[None, :, 0], gates[None, :, 1])
    pick = spread(chosen, 1.0)
    pick_gate = spread(chosen, gate_of[:, :, None, None, :])
    pick_a = spread(chosen & hit_a[:, :, None, :], 1.0)
    pick_b = spread(chosen & hit_b[:, :, None, :], 1.0)

    def hand_out(picker, parts):
        sent = bf16(dot(picker, jnp.concatenate(parts), ((1,), (0,))))
        sent = sent.reshape(len(destinations), sources * CAP, width)
        return jnp.concatenate(
            [sent[k] if k == 0 else move(sent[k], x_by(*to)) for k, to in enumerate(destinations)]
        )

    in_rows = hand_out(pick, [tokens, tok_near, tok_far, tok_last])
    grad_rows = hand_out(pick_gate, [grad_out, grad_near, grad_far, grad_last])

    gate_pre = dot(in_rows, full_gate, ((1,), (0,)))
    up_pre = dot(in_rows, full_up, ((1,), (0,)))
    sig = jax.nn.sigmoid(gate_pre)
    act = gate_pre * sig
    hidden = act * up_pre
    scaled = dot(grad_rows, full_down, ((1,), (0,)))
    route_grad = jnp.sum(scaled * hidden, axis=1)
    up_delta = bf16(scaled * act)
    gate_delta = bf16(scaled * up_pre * sig * (1.0 + gate_pre * (1.0 - sig)))

    def reduce_shares(left, right):
        share = bf16(dot(left, right, ((0,), (0,)))).reshape(2, NY, shard, hidden_units)

        def towards(dy):
            return lax.dynamic_index_in_dim(share, (y + dy) % NY, 1, False)

        far = towards(2)
        top = move(far[:, :half], y_by(1))
        low = move(far[:, half:], y_by(-1))
        up_one, down_one = towards(1), towards(NY - 1)
        up_one = jnp.concatenate([bf16(f32(up_one[:, :half]) + f32(top)), up_one[:, half:]], axis=1)
        down_one = jnp.concatenate([down_one[:, :half], bf16(f32(down_one[:, half:]) + f32(low))], axis=1)
        total = f32(towards(0)) + f32(move(up_one, y_by(1))) + f32(move(down_one, y_by(-1)))
        theirs = move(bf16(lax.dynamic_index_in_dim(total, 1 - z_lo, 0, False)), twin)
        return bf16(lax.dynamic_index_in_dim(total, z_lo, 0, False) + f32(theirs))

    grad_down = reduce_shares(grad_rows, bf16(hidden)).T[None]
    slot_dx = bf16(
        dot(gate_delta, full_gate, ((1,), (1,))) + dot(up_delta, full_up, ((1,), (1,)))
    )
    grad_gate = reduce_shares(in_rows, gate_delta)[None]
    grad_up = reduce_shares(in_rows, up_delta)[None]

    extra = 128
    slot_back = jnp.concatenate(
        [slot_dx, jnp.broadcast_to(bf16(route_grad)[:, None], (slot_dx.shape[0], extra))], axis=1
    ).reshape(len(destinations), sources * CAP, width + extra)
    back = jnp.concatenate(
        [
            slot_back[k] if k == 0 else move(slot_back[k], x_by(-dx, flip))
            for k, (dx, flip) in enumerate(destinations)
        ]
    )
    lane = jnp.arange(extra)[None, :]
    back_dx = bf16(dot(pick, back[:, :width], ((0,), (0,))))
    back_a = dot(pick_a, back[:, width:], ((0,), (0,)))
    back_b = dot(pick_b, back[:, width:], ((0,), (0,)))
    back_gate = bf16(jnp.where(lane == 0, back_a, back_b))
    parts = jnp.concatenate([back_dx, back_gate], axis=1).reshape(sources, rows, width + extra)
    for_last = move(parts[3], backward)
    for_far = move(parts[2], backward)
    near = move(bf16(f32(parts[1]) + f32(for_last)), across)
    whole = f32(parts[0]) + f32(for_far) + f32(near)
    d_tokens = bf16(whole[:, :width])
    own_gate = f32(gate_fixed) / 256.0
    d_gates = bf16(whole[:, width : width + 2] / own_gate)
    return d_tokens, d_gates, grad_gate, grad_up, grad_down


def solution(mesh):
    rows = P(("dp", "expert"), None)
    return jax.shard_map(
        local,
        mesh=mesh,
        in_specs=(
            rows,
            rows,
            rows,
            rows,
            P(("dp", "expert")),
            P("expert", "dp", None),
            P("expert", "dp", None),
            P("expert", None, "dp"),
        ),
        out_specs=(
            rows,
            rows,
            P("expert", "dp", None),
            P("expert", "dp", None),
            P("expert", None, "dp"),
        ),
        check_vma=False,
    )
```

time: 471 us -> 371 us (0.79); the launches traced: 470 us -> 365 us
  waiting for transfers between devices: 333 us -> 174 us
  starting transfers between devices: 51.5 us -> 91.5 us
  local copies, waits for them, and re-layouts: 31 us -> 47.4 us
  between operations: 14.7 us -> 2.79 us
  other arithmetic: 10.2 us -> 21.6 us
    ppermute x0 -> x56, waiting for transfers between devices: none -> 174 us  [move(): return lax.ppermute(array, ALL, pairs)]
    all_gather x4 -> x0, waiting for transfers between devices: 151 us -> none  [the longest x1 54.5 us: local(): lax.all_gather(local_up, 'dp', axis=0, tiled=True)]
    all_to_all x5 -> x0, waiting for transfers between devices: 126 us -> none  [the longest x1 70.9 us: local(): lax.all_to_all(slot_dx.reshape(experts, capacity, feature_width), 'expert...]
    ppermute x0 -> x56, starting transfers between devices: none -> 91.5 us  [move(): return lax.ppermute(array, ALL, pairs)]
    reduce_scatter x1 -> x0, waiting for transfers between devices: 53.5 us -> none  [local(): lax.psum_scatter(jnp.concatenate([contract_first(inputs_rows, gate_delta)...]
    all_to_all x5 -> x0, starting transfers between devices: 51.1 us -> none  [the longest x1 12.7 us: local(): lax.all_to_all(route_grad.reshape(experts, capacity), 'expert', split_axi...]
    scatter x3 -> x0, local copies, waits for them, and re-layouts: 16.3 us -> none  [the longest x1 7.16 us: local(): grads_send = jnp.zeros((slot_total, feature_width), jnp.bfloat16).at[slot...]
    dynamic_update_slice x0 -> x12, local copies, waits for them, and re-layouts: none -> 12.5 us  [the longest x8 9.07 us: local(): whole = lax.dynamic_update_slice(whole, block[at], (start, 0))]
  transfers between devices with their start and end apart: 10 -> 56, of which waited for: 8 -> 28; matrix products, arithmetic and copies ran while one was open for 14% -> 16% of each run, Pallas kernels for 0% -> 0%
where the time goes in v1:
time: 371 us; the launch traced here: 365 us
  waiting for transfers between devices  174 us (47%)
  starting transfers between devices  91.5 us (25%)
  local copies, waits for them, and re-layouts  47.4 us (13%)
  matrix products  27.9 us (8%)
  other arithmetic  21.6 us (6%)
    ppermute x56, waiting for transfers between devices, move(): return lax.ppermute(array, ALL, pairs)  174 us
    ppermute x56, starting transfers between devices, move(): return lax.ppermute(array, ALL, pairs)  91.5 us
    dot_general x14, matrix products, dot(): lax.dot_general(left, right, (dims, ((), ())), preferred_element_type=jnp...  27.9 us
    unnamed x114, local copies, waits for them, and re-layouts  14.6 us
    dynamic_update_slice x8, local copies, waits for them, and re-layouts, local(): whole = lax.dynamic_update_slice(whole, block[at], (start, 0))  9.07 us
  transfers between devices with their start and end apart: 56, of which 28 were waited for; matrix products, arithmetic and copies ran while one was open for 16% of the time, Pallas kernels for 0%

profile of v1, /device:TPU:1, one launch (start us, length us, event | category | flops | bytes accessed | tf_op | source)
XLA Modules:
  0.0 364.9 jit_solution(8418625892360687977)
XLA Ops:
  5.3 3.6 collective-permute-start.13
  11.2 4.8 %collective-permute-start = (s32[4,128]{1,0:T(4,128)S(1)}, s32[4,128]{1,0:T(4,128)S(1)}, u32[]{:S(2)}, u32[]{:S(2)}) collective-permute-start(s32[4,128]{1,0:T(4,128)S(1)} %get-tuple-element.101), channel_id=1, source_target_pairs={{0,152},{1,153},{2,154},{3,155},{4,156},{5,157},{6,158},{7,159},{8... | collective-permute-start | bytes 6152 | tf_op jit(solution)/shard_map/ppermute | solution.py:27
  23.5 17.1 %collective-permute-done.1 = s32[2,4,128]{2,1,0:T(4,128)S(1)} collective-permute-done((s32[2,4,128]{2,1,0:T(4,128)S(1)}, s32[2,4,128]{2,1,0:T(4,128)S(1)}, u32[]{:S(2)}, u32[]{:S(2)}) %collective-permute-start.1) | collective-permute-done | bytes 4128 | tf_op jit(solution)/shard_map/ppermute | solution.py:27
  46.0 8.3 %collective-permute-done.22 = bf16[128,2048]{1,0:T(8,128)(2,1)S(1)} collective-permute-done((bf16[128,2048]{1,0:T(8,128)(2,1)}, bf16[128,2048]{1,0:T(8,128)(2,1)S(1)}, u32[]{:S(2)}, u32[]{:S(2)}) %collective-permute-start.22) | collective-permute-done | bytes 524320 | tf_op jit(solution)/shard_map/ppermute | solution.py:27
  54.2 11.3 %collective-permute-done.23 = bf16[128,2048]{1,0:T(8,128)(2,1)S(1)} collective-permute-done((bf16[128,2048]{1,0:T(8,128)(2,1)}, bf16[128,2048]{1,0:T(8,128)(2,1)S(1)}, u32[]{:S(2)}, u32[]{:S(2)}) %collective-permute-start.23) | collective-permute-done | bytes 524320 | tf_op jit(solution)/shard_map/ppermute | solution.py:27
  68.3 3.2 collective-permute-start.24
  82.4 4.9 %collective-permute-done.26 = bf16[64,2048]{1,0:T(8,128)(2,1)S(1)} collective-permute-done((bf16[64,2048]{1,0:T(8,128)(2,1)S(1)}, bf16[64,2048]{1,0:T(8,128)(2,1)S(1)}, u32[]{:S(2)}, u32[]{:S(2)}) %collective-permute-start.26) | collective-permute-done | bytes 262176 | tf_op jit(solution)/shard_map/ppermute | solution.py:27
  88.5 4.9 %collective-permute-done.27 = bf16[64,2048]{1,0:T(8,128)(2,1)S(1)} collective-permute-done((bf16[64,2048]{1,0:T(8,128)(2,1)S(1)}, bf16[64,2048]{1,0:T(8,128)(2,1)S(1)}, u32[]{:S(2)}, u32[]{:S(2)}) %collective-permute-start.27) | collective-permute-done | bytes 262176 | tf_op jit(solution)/shard_map/ppermute | solution.py:27
  95.7 3.3 collective-permute-done.28
  103.6 3.7 %collective-permute-done.30 = bf16[64,2048]{1,0:T(8,128)(2,1)S(1)} collective-permute-done((bf16[64,2048]{1,0:T(8,128)(2,1)S(1)}, bf16[64,2048]{1,0:T(8,128)(2,1)S(1)}, u32[]{:S(2)}, u32[]{:S(2)}) %collective-permute-start.30) | collective-permute-done | bytes 262176 | tf_op jit(solution)/shard_map/ppermute | solution.py:27
  109.8 4.2 %collective-permute-done.5 = bf16[128,2048]{1,0:T(8,128)(2,1)S(1)} collective-permute-done((bf16[128,2048]{1,0:T(8,128)(2,1)S(1)}, bf16[128,2048]{1,0:T(8,128)(2,1)S(1)}, u32[]{:S(2)}, u32[]{:S(2)}) %collective-permute-start.5) | collective-permute-done | bytes 524320 | tf_op jit(solution)/shard_map/ppermute | solution.py:27
  119.0 15.2 %collective-permute-start.8 = (bf16[64,2048]{1,0:T(8,128)(2,1)S(1)}, bf16[64,2048]{1,0:T(8,128)(2,1)S(1)}, u32[]{:S(2)}, u32[]{:S(2)}) collective-permute-start(bf16[64,2048]{1,0:T(8,128)(2,1)S(1)} %get-tuple-element.54), channel_id=1, source_target_pairs={{0,3},{1,2},{2,5},{3,4},{4,7},{5,6},{6,1},{7,0},{8,11},{9,10},{10,... | collective-permute-start | bytes 786440 | tf_op jit(solution)/shard_map/ppermute | solution.py:27
  144.3 4.5 %collective-permute-done.9 = bf16[64,2048]{1,0:T(8,128)(2,1)S(1)} collective-permute-done((bf16[64,2048]{1,0:T(8,128)(2,1)S(1)}, bf16[64,2048]{1,0:T(8,128)(2,1)S(1)}, u32[]{:S(2)}, u32[]{:S(2)}) %collective-permute-start.9) | collective-permute-done | bytes 262176 | tf_op jit(solution)/shard_map/ppermute | solution.py:27
  154.2 5.2 %collective-permute-done.11 = bf16[64,2048]{1,0:T(8,128)(2,1)S(1)} collective-permute-done((bf16[64,2048]{1,0:T(8,128)(2,1)S(1)}, bf16[64,2048]{1,0:T(8,128)(2,1)S(1)}, u32[]{:S(2)}, u32[]{:S(2)}) %collective-permute-start.11) | collective-permute-done | bytes 262176 | tf_op jit(solution)/shard_map/ppermute | solution.py:27
  161.5 3.7 %collective-permute-done.12 = bf16[64,2048]{1,0:T(8,128)(2,1)S(1)} collective-permute-done((bf16[64,2048]{1,0:T(8,128)(2,1)S(1)}, bf16[64,2048]{1,0:T(8,128)(2,1)S(1)}, u32[]{:S(2)}, u32[]{:S(2)}) %collective-permute-start.12) | collective-permute-done | bytes 262176 | tf_op jit(solution)/shard_map/ppermute | solution.py:27
  170.3 3.9 %collective-permute-done.21 = bf16[3,128,768]{1,2,0:T(8,128)(2,1)S(1)} collective-permute-done((bf16[3,128,768]{1,2,0:T(8,128)(2,1)S(1)}, bf16[3,128,768]{1,2,0:T(8,128)(2,1)S(1)}, u32[]{:S(2)}, u32[]{:S(2)}) %collective-permute-start.21) | collective-permute-done | bytes 589856 | tf_op jit(solution)/shard_map/ppermute | solution.py:27
  182.4 5.2 %multiply_convert_fusion.1 = (bf16[512,768]{1,0:T(8,128)(2,1)}, bf16[512]{0:T(512)(128)(2,1)S(1)}, bf16[512,768]{1,0:T(8,128)(2,1)S(1)}) fusion(f32[512,768]{1,0:T(8,128)S(1)} %fusion.103, f32[512,768]{1,0:T(8,128)S(1)} %fusion.102, bf16[512,2048]{1,0:T(8,128)(2,1)S(1)} %constant_dynamic-update-slice_fusion, bf16[2048,768]{0,1:T(8,128)(2,1)} %get-tuple-element.60), kind=kOutput, calls=%fused_computation.43 | convolution fusion | flops 1616903680 | bytes 9962496 | tf_op jit(solution)/shard_map/dot_general | solution.py:55
  189.5 3.7 %fusion.104 = f32[512,2048]{1,0:T(8,128)} fusion(bf16[512,768]{1,0:T(8,128)(2,1)S(1)} %get-tuple-element.31, bf16[2048,768]{0,1:T(8,128)(2,1)S(1)} %copy-done.14), kind=kOutput, calls=%fused_computation.248 | convolution fusion | flops 1610612736 | bytes 8126464 | tf_op jit(solution)/shard_map/dot_general | solution.py:55
  203.1 3.7 %convolution_convert_fusion.2 = bf16[2048,768]{1,0:T(8,128)(2,1)S(1)} fusion(bf16[512,2048]{1,0:T(8,128)(2,1)} %copy-done.38, bf16[512,768]{1,0:T(8,128)(2,1)} %get-tuple-element.19), kind=kOutput, calls=%fused_computation.13 | convolution fusion | flops 1612185600 | bytes 6029312 | tf_op jit(solution)/shard_map/dot_general | solution.py:55
  228.2 4.4 %collective-permute-done.32 = bf16[64,2176]{1,0:T(8,128)(2,1)S(1)} collective-permute-done((bf16[64,2176]{1,0:T(8,128)(2,1)S(1)}, bf16[64,2176]{1,0:T(8,128)(2,1)S(1)}, u32[]{:S(2)}, u32[]{:S(2)}) %collective-permute-start.32) | collective-permute-done | bytes 278560 | tf_op jit(solution)/shard_map/ppermute | solution.py:27
  232.7 4.7 %collective-permute-start.33 = (bf16[64,2176]{1,0:T(8,128)(2,1)S(1)}, bf16[64,2176]{1,0:T(8,128)(2,1)S(1)}, u32[]{:S(2)}, u32[]{:S(2)}) collective-permute-start(bf16[64,2176]{1,0:T(8,128)(2,1)S(1)} %copy-done.35), channel_id=1, source_target_pairs={{0,7},{1,6},{2,1},{3,0},{4,3},{5,2},{6,5},{7,4},{8,15},{9,14},{10,... | collective-permute-start | bytes 835592 | tf_op jit(solution)/shard_map/ppermute | solution.py:27
  237.4 5.7 %collective-permute-done.33 = bf16[64,2176]{1,0:T(8,128)(2,1)S(1)} collective-permute-done((bf16[64,2176]{1,0:T(8,128)(2,1)S(1)}, bf16[64,2176]{1,0:T(8,128)(2,1)S(1)}, u32[]{:S(2)}, u32[]{:S(2)}) %collective-permute-start.33) | collective-permute-done | bytes 278560 | tf_op jit(solution)/shard_map/ppermute | solution.py:27
  244.7 8.3 %collective-permute-done.34 = bf16[64,2176]{1,0:T(8,128)(2,1)S(1)} collective-permute-done((bf16[64,2176]{1,0:T(8,128)(2,1)S(1)}, bf16[64,2176]{1,0:T(8,128)(2,1)S(1)}, u32[]{:S(2)}, u32[]{:S(2)}) %collective-permute-start.34) | collective-permute-done | bytes 278560 | tf_op jit(solution)/shard_map/ppermute | solution.py:27
  255.2 8.6 %collective-permute-done.35 = bf16[64,2176]{1,0:T(8,128)(2,1)S(1)} collective-permute-done((bf16[64,2176]{1,0:T(8,128)(2,1)S(1)}, bf16[64,2176]{1,0:T(8,128)(2,1)S(1)}, u32[]{:S(2)}, u32[]{:S(2)}) %collective-permute-start.35) | collective-permute-done | bytes 278560 | tf_op jit(solution)/shard_map/ppermute | solution.py:27
  263.8 9.0 %collective-permute-done.36 = bf16[64,2176]{1,0:T(8,128)(2,1)S(1)} collective-permute-done((bf16[64,2176]{1,0:T(8,128)(2,1)S(1)}, bf16[64,2176]{1,0:T(8,128)(2,1)S(1)}, u32[]{:S(2)}, u32[]{:S(2)}) %collective-permute-start.36) | collective-permute-done | bytes 278560 | tf_op jit(solution)/shard_map/ppermute | solution.py:27
  272.8 9.9 %collective-permute-done.37 = bf16[64,2176]{1,0:T(8,128)(2,1)S(1)} collective-permute-done((bf16[64,2176]{1,0:T(8,128)(2,1)S(1)}, bf16[64,2176]{1,0:T(8,128)(2,1)S(1)}, u32[]{:S(2)}, u32[]{:S(2)}) %collective-permute-start.37) | collective-permute-done | bytes 278560 | tf_op jit(solution)/shard_map/ppermute | solution.py:27
  288.9 3.3 collective-permute-start.39
  297.3 5.4 %collective-permute-done.39 = bf16[128,2176]{0,1:T(8,128)(2,1)S(1)} collective-permute-done((bf16[128,2176]{0,1:T(8,128)(2,1)S(1)}, bf16[128,2176]{0,1:T(8,128)(2,1)S(1)}, u32[]{:S(2)}, u32[]{:S(2)}) %collective-permute-start.39) | collective-permute-done | bytes 557088 | tf_op jit(solution)/shard_map/ppermute | solution.py:27
  303.8 8.6 %collective-permute-done.52 = bf16[2,256,768]{1,2,0:T(8,128)(2,1)S(1)} collective-permute-done((bf16[2,256,768]{1,2,0:T(8,128)(2,1)S(1)}, bf16[2,256,768]{1,2,0:T(8,128)(2,1)S(1)}, u32[]{:S(2)}, u32[]{:S(2)}) %collective-permute-start.52) | collective-permute-done | bytes 786464 | tf_op jit(solution)/shard_map/ppermute | solution.py:27
  315.4 13.8 %collective-permute-done.47 = bf16[2,256,768]{2,1,0:T(8,128)(2,1)S(1)} collective-permute-done((bf16[2,256,768]{2,1,0:T(8,128)(2,1)S(1)}, bf16[2,256,768]{2,1,0:T(8,128)(2,1)S(1)}, u32[]{:S(2)}, u32[]{:S(2)}) %collective-permute-start.47) | collective-permute-done | bytes 786464 | tf_op jit(solution)/shard_map/ppermute | solution.py:27
  333.8 12.3 %collective-permute-done.42 = bf16[2,256,768]{2,1,0:T(8,128)(2,1)S(1)} collective-permute-done((bf16[2,256,768]{2,1,0:T(8,128)(2,1)S(1)}, bf16[2,256,768]{2,1,0:T(8,128)(2,1)S(1)}, u32[]{:S(2)}, u32[]{:S(2)}) %collective-permute-start.42) | collective-permute-done | bytes 786464 | tf_op jit(solution)/shard_map/ppermute | solution.py:27
  359.3 3.7 %collective-permute-done.45 = bf16[256,768]{1,0:T(8,128)(2,1)} collective-permute-done((bf16[256,768]{1,0:T(8,128)(2,1)}, bf16[256,768]{1,0:T(8,128)(2,1)}, u32[]{:S(2)}, u32[]{:S(2)}) %collective-permute-start.45) | collective-permute-done | bytes 393248 | tf_op jit(solution)/shard_map/ppermute | solution.py:27
  (296 shorter events, 150.0 us)
Async XLA Ops:
  5.3 66.2 %collective-permute-start.13 = (bf16[3,256,768]{1,2,0:T(8,128)(2,1)}, bf16[3,256,768]{1,2,0:T(8,128)(2,1)}, u32[]{:S(2)}, u32[]{:S(2)}) collective-permute-start(bf16[3,256,768]{1,2,0:T(8,128)(2,1)} %pad_maximum_fusion), channel_id=1, source_target_pairs={{0,96},{1,97},{2,98},{3,99},{4,100},{5,101},{6,102},{7,103},{8,104... | collective-permute-start | bytes 3538952 | tf_op jit(solution)/shard_map/ppermute | solution.py:27
  8.8 67.4 %collective-permute-start.14 = (bf16[3,256,768]{1,2,0:T(8,128)(2,1)}, bf16[3,256,768]{1,2,0:T(8,128)(2,1)}, u32[]{:S(2)}, u32[]{:S(2)}) collective-permute-start(bf16[3,256,768]{1,2,0:T(8,128)(2,1)} %pad_maximum_fusion), channel_id=1, source_target_pairs={{0,32},{1,33},{2,34},{3,35},{4,36},{5,37},{6,38},{7,39},{8,40},{9,... | collective-permute-start | bytes 3538952 | tf_op jit(solution)/shard_map/ppermute | solution.py:27
  8.8 92.0 %collective-permute-start.17 = (bf16[3,256,768]{1,2,0:T(8,128)(2,1)}, bf16[3,256,768]{1,2,0:T(8,128)(2,1)}, u32[]{:S(2)}, u32[]{:S(2)}) collective-permute-start(bf16[3,256,768]{1,2,0:T(8,128)(2,1)} %pad_maximum_fusion), channel_id=1, source_target_pairs={{0,128},{1,129},{2,130},{3,131},{4,132},{5,133},{6,134},{7,135},{8... | collective-permute-start | bytes 3538952 | tf_op jit(solution)/shard_map/ppermute | solution.py:27
  16.0 28.0 %collective-permute-start.2 = (bf16[128,2048]{1,0:T(8,128)(2,1)}, bf16[128,2048]{1,0:T(8,128)(2,1)}, u32[]{:S(2)}, u32[]{:S(2)}) collective-permute-start(bf16[128,2048]{1,0:T(8,128)(2,1)} %param.8), channel_id=1, source_target_pairs={{0,152},{1,153},{2,154},{3,155},{4,156},{5,157},{6,158},{7,159},{8... | collective-permute-start | bytes 1572872 | tf_op jit(solution)/shard_map/ppermute | solution.py:27
  23.2 17.5 %collective-permute-start.1 = (s32[2,4,128]{2,1,0:T(4,128)S(1)}, s32[2,4,128]{2,1,0:T(4,128)S(1)}, u32[]{:S(2)}, u32[]{:S(2)}) collective-permute-start(s32[2,4,128]{2,1,0:T(4,128)S(1)} %pad_add_fusion.2), channel_id=1, source_target_pairs={{0,8},{1,9},{2,10},{3,11},{4,12},{5,13},{6,14},{7,15},{8,16},{9,17... | collective-permute-start | bytes 12296 | tf_op jit(solution)/shard_map/ppermute | solution.py:27
  44.0 21.6 %collective-permute-start.23 = (bf16[128,2048]{1,0:T(8,128)(2,1)}, bf16[128,2048]{1,0:T(8,128)(2,1)S(1)}, u32[]{:S(2)}, u32[]{:S(2)}) collective-permute-start(bf16[128,2048]{1,0:T(8,128)(2,1)} %collective-permute-done.2), channel_id=1, source_target_pairs={{0,8},{1,9},{2,10},{3,11},{4,12},{5,13},{6,14},{7,15},{8,16},{9,17... | collective-permute-start | bytes 1572872 | tf_op jit(solution)/shard_map/ppermute | solution.py:27
  54.2 39.1 %collective-permute-start.3 = (bf16[128,2048]{1,0:T(8,128)(2,1)S(1)}, bf16[128,2048]{1,0:T(8,128)(2,1)S(1)}, u32[]{:S(2)}, u32[]{:S(2)}) collective-permute-start(bf16[128,2048]{1,0:T(8,128)(2,1)S(1)} %copy-done.42), channel_id=1, source_target_pairs={{0,152},{1,153},{2,154},{3,155},{4,156},{5,157},{6,158},{7,159},{8... | collective-permute-start | bytes 1572872 | tf_op jit(solution)/shard_map/ppermute | solution.py:27
  76.2 33.5 %collective-permute-start.4 = (bf16[128,2048]{1,0:T(8,128)(2,1)S(1)}, bf16[128,2048]{1,0:T(8,128)(2,1)S(1)}, u32[]{:S(2)}, u32[]{:S(2)}) collective-permute-start(bf16[128,2048]{1,0:T(8,128)(2,1)S(1)} %copy-done.42), channel_id=1, source_target_pairs={{0,8},{1,9},{2,10},{3,11},{4,12},{5,13},{6,14},{7,15},{8,16},{9,17... | collective-permute-start | bytes 1572872 | tf_op jit(solution)/shard_map/ppermute | solution.py:27
  99.0 15.0 %collective-permute-start.5 = (bf16[128,2048]{1,0:T(8,128)(2,1)S(1)}, bf16[128,2048]{1,0:T(8,128)(2,1)S(1)}, u32[]{:S(2)}, u32[]{:S(2)}) collective-permute-start(bf16[128,2048]{1,0:T(8,128)(2,1)S(1)} %collective-permute-done.3), channel_id=1, source_target_pairs={{0,8},{1,9},{2,10},{3,11},{4,12},{5,13},{6,14},{7,15},{8,16},{9,17... | collective-permute-start | bytes 1572872 | tf_op jit(solution)/shard_map/ppermute | solution.py:27
  100.9 16.1 %collective-permute-start.15 = (bf16[3,128,768]{1,2,0:T(8,128)(2,1)S(1)}, bf16[3,128,768]{1,2,0:T(8,128)(2,1)S(1)}, u32[]{:S(2)}, u32[]{:S(2)}) collective-permute-start(bf16[3,128,768]{1,2,0:T(8,128)(2,1)S(1)} %slice.385), channel_id=1, source_target_pairs={{0,32},{1,33},{2,34},{3,35},{4,36},{5,37},{6,38},{7,39},{8,40},{9,... | collective-permute-start | bytes 1769480 | tf_op jit(solution)/shard_map/ppermute | solution.py:27
  100.9 18.1 %collective-permute-start.16 = (bf16[3,128,768]{1,2,0:T(8,128)(2,1)S(1)}, bf16[3,128,768]{1,2,0:T(8,128)(2,1)S(1)}, u32[]{:S(2)}, u32[]{:S(2)}) collective-permute-start(bf16[3,128,768]{1,2,0:T(8,128)(2,1)S(1)} %slice.387), channel_id=1, source_target_pairs={{0,96},{1,97},{2,98},{3,99},{4,100},{5,101},{6,102},{7,103},{8,104... | collective-permute-start | bytes 1769480 | tf_op jit(solution)/shard_map/ppermute | solution.py:27
  107.3 52.1 %collective-permute-start.18 = (bf16[3,256,768]{1,2,0:T(8,128)(2,1)}, bf16[3,256,768]{1,2,0:T(8,128)(2,1)S(1)}, u32[]{:S(2)}, u32[]{:S(2)}) collective-permute-start(bf16[3,256,768]{1,2,0:T(8,128)(2,1)} %collective-permute-done.17), channel_id=1, source_target_pairs={{0,96},{1,97},{2,98},{3,99},{4,100},{5,101},{6,102},{7,103},{8,104... | collective-permute-start | bytes 3538952 | tf_op jit(solution)/shard_map/ppermute | solution.py:27
  109.7 44.2 %collective-permute-start.19 = (bf16[3,256,768]{1,2,0:T(8,128)(2,1)}, bf16[3,256,768]{1,2,0:T(8,128)(2,1)S(1)}, u32[]{:S(2)}, u32[]{:S(2)}) collective-permute-start(bf16[3,256,768]{1,2,0:T(8,128)(2,1)} %collective-permute-done.17), channel_id=1, source_target_pairs={{0,32},{1,33},{2,34},{3,35},{4,36},{5,37},{6,38},{7,39},{8,40},{9,... | collective-permute-start | bytes 3538952 | tf_op jit(solution)/shard_map/ppermute | solution.py:27
  115.4 23.9 %collective-permute-start.6 = (bf16[64,2048]{1,0:T(8,128)(2,1)S(1)}, bf16[64,2048]{1,0:T(8,128)(2,1)S(1)}, u32[]{:S(2)}, u32[]{:S(2)}) collective-permute-start(bf16[64,2048]{1,0:T(8,128)(2,1)S(1)} %get-tuple-element.56), channel_id=1, source_target_pairs={{0,1},{1,0},{2,3},{3,2},{4,5},{5,4},{6,7},{7,6},{8,9},{9,8},{10,11... | collective-permute-start | bytes 786440 | tf_op jit(solution)/shard_map/ppermute | solution.py:27
  116.9 25.0 %collective-permute-start.7 = (bf16[64,2048]{1,0:T(8,128)(2,1)S(1)}, bf16[64,2048]{1,0:T(8,128)(2,1)S(1)}, u32[]{:S(2)}, u32[]{:S(2)}) collective-permute-start(bf16[64,2048]{1,0:T(8,128)(2,1)S(1)} %get-tuple-element.55), channel_id=1, source_target_pairs={{0,2},{1,3},{2,4},{3,5},{4,6},{5,7},{6,0},{7,1},{8,10},{9,11},{10,... | collective-permute-start | bytes 786440 | tf_op jit(solution)/shard_map/ppermute | solution.py:27
  119.0 23.7 %collective-permute-start.8 = (bf16[64,2048]{1,0:T(8,128)(2,1)S(1)}, bf16[64,2048]{1,0:T(8,128)(2,1)S(1)}, u32[]{:S(2)}, u32[]{:S(2)}) collective-permute-start(bf16[64,2048]{1,0:T(8,128)(2,1)S(1)} %get-tuple-element.54), channel_id=1, source_target_pairs={{0,3},{1,2},{2,5},{3,4},{4,7},{5,6},{6,1},{7,0},{8,11},{9,10},{10,... | collective-permute-start | bytes 786440 | tf_op jit(solution)/shard_map/ppermute | solution.py:27
  142.7 16.7 %collective-permute-start.11 = (bf16[64,2048]{1,0:T(8,128)(2,1)S(1)}, bf16[64,2048]{1,0:T(8,128)(2,1)S(1)}, u32[]{:S(2)}, u32[]{:S(2)}) collective-permute-start(bf16[64,2048]{1,0:T(8,128)(2,1)S(1)} %get-tuple-element.51), channel_id=1, source_target_pairs={{0,6},{1,7},{2,0},{3,1},{4,2},{5,3},{6,4},{7,5},{8,14},{9,15},{10,... | collective-permute-start | bytes 786440 | tf_op jit(solution)/shard_map/ppermute | solution.py:27
  148.8 16.5 %collective-permute-start.12 = (bf16[64,2048]{1,0:T(8,128)(2,1)S(1)}, bf16[64,2048]{1,0:T(8,128)(2,1)S(1)}, u32[]{:S(2)}, u32[]{:S(2)}) collective-permute-start(bf16[64,2048]{1,0:T(8,128)(2,1)S(1)} %get-tuple-element.50), channel_id=1, source_target_pairs={{0,7},{1,6},{2,1},{3,0},{4,3},{5,2},{6,5},{7,4},{8,15},{9,14},{10,... | collective-permute-start | bytes 786440 | tf_op jit(solution)/shard_map/ppermute | solution.py:27
  154.1 15.3 %collective-permute-start.20 = (bf16[3,128,768]{1,2,0:T(8,128)(2,1)S(1)}, bf16[3,128,768]{1,2,0:T(8,128)(2,1)S(1)}, u32[]{:S(2)}, u32[]{:S(2)}) collective-permute-start(bf16[3,128,768]{1,2,0:T(8,128)(2,1)S(1)} %slice.392), channel_id=1, source_target_pairs={{0,32},{1,33},{2,34},{3,35},{4,36},{5,37},{6,38},{7,39},{8,40},{9,... | collective-permute-start | bytes 1769480 | tf_op jit(solution)/shard_map/ppermute | solution.py:27
  199.2 85.8 %collective-permute-start.51 = (bf16[2,128,768]{1,2,0:T(8,128)(2,1)}, bf16[2,128,768]{1,2,0:T(8,128)(2,1)}, u32[]{:S(2)}, u32[]{:S(2)}) collective-permute-start(bf16[2,128,768]{1,2,0:T(8,128)(2,1)} %get-tuple-element.73), channel_id=1, source_target_pairs={{0,32},{1,33},{2,34},{3,35},{4,36},{5,37},{6,38},{7,39},{8,40},{9,... | collective-permute-start | bytes 1179656 | tf_op jit(solution)/shard_map/ppermute | solution.py:27
  200.0 88.9 %collective-permute-start.53 = (bf16[2,128,768]{1,2,0:T(8,128)(2,1)}, bf16[2,128,768]{1,2,0:T(8,128)(2,1)}, u32[]{:S(2)}, u32[]{:S(2)}) collective-permute-start(bf16[2,128,768]{1,2,0:T(8,128)(2,1)} %get-tuple-element.74), channel_id=1, source_target_pairs={{0,96},{1,97},{2,98},{3,99},{4,100},{5,101},{6,102},{7,103},{8,104... | collective-permute-start | bytes 1179656 | tf_op jit(solution)/shard_map/ppermute | solution.py:27
  220.8 72.5 %collective-permute-start.46 = (bf16[2,128,768]{2,1,0:T(8,128)(2,1)}, bf16[2,128,768]{2,1,0:T(8,128)(2,1)S(1)}, u32[]{:S(2)}, u32[]{:S(2)}) collective-permute-start(bf16[2,128,768]{2,1,0:T(8,128)(2,1)} %get-tuple-element.75), channel_id=1, source_target_pairs={{0,32},{1,33},{2,34},{3,35},{4,36},{5,37},{6,38},{7,39},{8,40},{9,... | collective-permute-start | bytes 1179656 | tf_op jit(solution)/shard_map/ppermute | solution.py:27
  221.9 71.9 %collective-permute-start.48 = (bf16[2,128,768]{2,1,0:T(8,128)(2,1)}, bf16[2,128,768]{2,1,0:T(8,128)(2,1)S(1)}, u32[]{:S(2)}, u32[]{:S(2)}) collective-permute-start(bf16[2,128,768]{2,1,0:T(8,128)(2,1)} %get-tuple-element.76), channel_id=1, source_target_pairs={{0,96},{1,97},{2,98},{3,99},{4,100},{5,101},{6,102},{7,103},{8,104... | collective-permute-start | bytes 1179656 | tf_op jit(solution)/shard_map/ppermute | solution.py:27
  293.4 56.7 %collective-permute-start.38 = (bf16[128,2176]{0,1:T(8,128)(2,1)S(1)}, bf16[128,2176]{0,1:T(8,128)(2,1)S(1)}, u32[]{:S(2)}, u32[]{:S(2)}) collective-permute-start(bf16[128,2176]{0,1:T(8,128)(2,1)S(1)} %get-tuple-element.32), channel_id=1, source_target_pairs={{0,24},{1,25},{2,26},{3,27},{4,28},{5,29},{6,30},{7,31},{8,0},{9,1... | collective-permute-start | bytes 1671176 | tf_op jit(solution)/shard_map/ppermute | solution.py:27
  293.8 18.6 %collective-permute-start.52 = (bf16[2,256,768]{1,2,0:T(8,128)(2,1)S(1)}, bf16[2,256,768]{1,2,0:T(8,128)(2,1)S(1)}, u32[]{:S(2)}, u32[]{:S(2)}) collective-permute-start(bf16[2,256,768]{1,2,0:T(8,128)(2,1)S(1)} %pad_maximum_fusion.5), channel_id=1, source_target_pairs={{0,32},{1,33},{2,34},{3,35},{4,36},{5,37},{6,38},{7,39},{8,40},{9,... | collective-permute-start | bytes 2359304 | tf_op jit(solution)/shard_map/ppermute | solution.py:27
  294.0 18.4 %collective-permute-start.54 = (bf16[2,256,768]{1,2,0:T(8,128)(2,1)S(1)}, bf16[2,256,768]{1,2,0:T(8,128)(2,1)S(1)}, u32[]{:S(2)}, u32[]{:S(2)}) collective-permute-start(bf16[2,256,768]{1,2,0:T(8,128)(2,1)S(1)} %pad_maximum_fusion.6), channel_id=1, source_target_pairs={{0,96},{1,97},{2,98},{3,99},{4,100},{5,101},{6,102},{7,103},{8,104... | collective-permute-start | bytes 2359304 | tf_op jit(solution)/shard_map/ppermute | solution.py:27
  297.0 32.2 %collective-permute-start.47 = (bf16[2,256,768]{2,1,0:T(8,128)(2,1)S(1)}, bf16[2,256,768]{2,1,0:T(8,128)(2,1)S(1)}, u32[]{:S(2)}, u32[]{:S(2)}) collective-permute-start(bf16[2,256,768]{2,1,0:T(8,128)(2,1)S(1)} %pad_maximum_fusion.3), channel_id=1, source_target_pairs={{0,32},{1,33},{2,34},{3,35},{4,36},{5,37},{6,38},{7,39},{8,40},{9,... | collective-permute-start | bytes 2359304 | tf_op jit(solution)/shard_map/ppermute | solution.py:27
  302.7 27.3 %collective-permute-start.49 = (bf16[2,256,768]{2,1,0:T(8,128)(2,1)S(1)}, bf16[2,256,768]{2,1,0:T(8,128)(2,1)S(1)}, u32[]{:S(2)}, u32[]{:S(2)}) collective-permute-start(bf16[2,256,768]{2,1,0:T(8,128)(2,1)S(1)} %pad_maximum_fusion.4), channel_id=1, source_target_pairs={{0,96},{1,97},{2,98},{3,99},{4,100},{5,101},{6,102},{7,103},{8,104... | collective-permute-start | bytes 2359304 | tf_op jit(solution)/shard_map/ppermute | solution.py:27
  312.3 33.7 %collective-permute-start.42 = (bf16[2,256,768]{2,1,0:T(8,128)(2,1)S(1)}, bf16[2,256,768]{2,1,0:T(8,128)(2,1)S(1)}, u32[]{:S(2)}, u32[]{:S(2)}) collective-permute-start(bf16[2,256,768]{2,1,0:T(8,128)(2,1)S(1)} %pad_maximum_fusion.1), channel_id=1, source_target_pairs={{0,32},{1,33},{2,34},{3,35},{4,36},{5,37},{6,38},{7,39},{8,40},{9,... | collective-permute-start | bytes 2359304 | tf_op jit(solution)/shard_map/ppermute | solution.py:27
  312.3 35.4 %collective-permute-start.44 = (bf16[2,256,768]{2,1,0:T(8,128)(2,1)S(1)}, bf16[2,256,768]{2,1,0:T(8,128)(2,1)S(1)}, u32[]{:S(2)}, u32[]{:S(2)}) collective-permute-start(bf16[2,256,768]{2,1,0:T(8,128)(2,1)S(1)} %pad_maximum_fusion.2), channel_id=1, source_target_pairs={{0,96},{1,97},{2,98},{3,99},{4,100},{5,101},{6,102},{7,103},{8,104... | collective-permute-start | bytes 2359304 | tf_op jit(solution)/shard_map/ppermute | solution.py:27
  329.2 20.9 %collective-permute-start.40 = (bf16[128,2176]{0,1:T(8,128)(2,1)S(1)}, bf16[128,2176]{0,1:T(8,128)(2,1)S(1)}, u32[]{:S(2)}, u32[]{:S(2)}) collective-permute-start(bf16[128,2176]{0,1:T(8,128)(2,1)S(1)} %add_convert_fusion.1), channel_id=1, source_target_pairs={{0,152},{1,153},{2,154},{3,155},{4,156},{5,157},{6,158},{7,159},{8... | collective-permute-start | bytes 1671176 | tf_op jit(solution)/shard_map/ppermute | solution.py:27
  329.9 25.7 %collective-permute-start.55 = (bf16[256,768]{0,1:T(8,128)(2,1)S(1)}, bf16[256,768]{0,1:T(8,128)(2,1)}, u32[]{:S(2)}, u32[]{:S(2)}) collective-permute-start(bf16[256,768]{0,1:T(8,128)(2,1)S(1)} %fusion.43), channel_id=1, source_target_pairs={{0,128},{1,129},{2,130},{3,131},{4,132},{5,133},{6,134},{7,135},{8... | collective-permute-start | bytes 1179656 | tf_op jit(solution)/shard_map/ppermute | solution.py:27
  (70 other events, 829.0 us)
